TPU v7x, 32 devices: a whole 2x2x4 slice. The times are simulated.
32 devices in a mesh: group: 4 (over z), dev: 8 (over y, x, core).
Axes of the slice: x: 2, y: 2, z: 4, core: 2. Of those that a mesh axis runs over, the one named last changes fastest.
Arguments:
- points: bfloat16 [131072, 64], P(('group', 'dev')), may hold values from -4 to 4
- weights: bfloat16 [131072, 64], P(('group', 'dev')), may hold values from -4 to 4
- near_leaves: int32 [256, 4], P(('group', 'dev')), may hold values from 0 to 63, as said below
- near_count: int32 [256], P(('group', 'dev')), may hold values from 1 to 4, as said below
- leaf_perm: int32 [256, 512], P(('group', 'dev')), may hold values from 0 to 511, each once within a row
- local_perm: int32 [32, 7, 512], P(('group', 'dev')), may hold values from 0 to 511, each once within a row
- upper_perm: int32 [30, 512], replicated, may hold values from 0 to 511, each once within a row
Outputs:
- product: float32 [131072, 64], P(('group', 'dev'))
Inputs may be any that keep to these rules, and one draw needn't show every extreme that they name: `near_leaves`: leaf numbers count within the leaf's own group. Entry 0 is the leaf itself; entries 1 to near_count - 1 are distinct other leaves held by the same device or by the device just before or after it along dev in the same group; later entries repeat the leaf itself. `near_count`: at least one leaf of every group has exactly 4 live entries. `leaf_perm`: each row holds every number of 0 to 511 once. `local_perm`: each row holds every number of 0 to 511 once. `upper_perm`: each row holds every number of 0 to 511 once.
All inputs are finite; a program needn't handle non-finite values.
Results may differ from a plain program's by a relative error of at most 0.0062.
Values may be sent and summed in bfloat16 or wider, within the bound.
A program may use at most 64 MiB of HBM per device.

v0:
```python
import jax
import jax.numpy as jnp
from jax import lax
from jax.sharding import PartitionSpec as P

spread_width = 10.0
merge_gain = 0.8408964152537145


def with_halo(block, sides, width):
    for axis, dim in sides:
        count = lax.axis_size(axis)
        forward = [(i, i + 1) for i in range(count - 1)]
        backward = [(target, source) for source, target in forward]
        low = lax.ppermute(
            lax.slice_in_dim(block, block.shape[dim] - width, None, axis=dim), axis, forward
        )
        high = lax.ppermute(lax.slice_in_dim(block, 0, width, axis=dim), axis, backward)
        block = jnp.concatenate([low, block, high], axis=dim)
    return block


def swapped(block, axis, stride):
    count = lax.axis_size(axis)
    route = []
    for low in range(count):
        high = low | 1 << stride
        if high != low and high < count:
            route += [(low, high), (high, low)]
    return lax.ppermute(block, axis, route)


def kernel_block(left, right):
    left_sq = jnp.sum(jnp.square(left.astype(jnp.float32)), axis=-1)
    right_sq = jnp.sum(jnp.square(right.astype(jnp.float32)), axis=-1)
    cross = lax.dot_general(
        left, right, (((1,), (1,)), ((), ())), preferred_element_type=jnp.float32
    )
    return jnp.exp(-(left_sq[:, None] + right_sq[None, :] - 2.0 * cross) / spread_width)


def pick_tables(ordering):
    total_rows = ordering.shape[0]
    skel_rows = total_rows // 2
    columns = jnp.arange(total_rows, dtype=jnp.int32)
    head_pick = ordering[:skel_rows, None] == columns[None, :]
    tail_pick = ordering[skel_rows:, None] == columns[None, :]
    return (head_pick, tail_pick)


def merge_node(stacked, ordering, feat_cols):
    head_pick, tail_pick = pick_tables(ordering)
    head_table = head_pick.astype(jnp.bfloat16)
    both_table = (head_pick | tail_pick).astype(jnp.bfloat16)
    coords = jnp.dot(head_table, stacked[:, :feat_cols], preferred_element_type=jnp.float32)
    summed = jnp.dot(both_table, stacked[:, feat_cols:], preferred_element_type=jnp.float32)
    merged = (merge_gain * summed).astype(jnp.bfloat16)
    return jnp.concatenate([coords.astype(jnp.bfloat16), merged], axis=1)


def far_term(own_rows, sibling, feat_cols):
    block = kernel_block(own_rows[:, :feat_cols], sibling[:, :feat_cols]).astype(jnp.bfloat16)
    return jnp.dot(block, sibling[:, feat_cols:], preferred_element_type=jnp.float32)


def expand(values, ordering):
    head_pick, tail_pick = pick_tables(ordering)
    both_table = (head_pick | tail_pick).astype(jnp.float32)
    return lax.dot_general(
        both_table,
        values,
        (((0,), (0,)), ((), ())),
        precision=lax.Precision.HIGHEST,
        preferred_element_type=jnp.float32,
    )


def near_field(stacked, window, near_leaves, near_count, feat_cols, first_leaf, loop_end):
    leaves_here = near_leaves.shape[0]
    leaf_rows = stacked.shape[0] // leaves_here
    rhs_cols = stacked.shape[1] - feat_cols
    own_coords = stacked.reshape(leaves_here, leaf_rows, stacked.shape[1])[:, :, :feat_cols]
    tiles = window.reshape(window.shape[0] // leaf_rows, leaf_rows, window.shape[1])
    own_sq = jnp.sum(jnp.square(own_coords.astype(jnp.float32)), axis=-1)

    def add_slot(slot_no, summed):
        place = lax.dynamic_index_in_dim(near_leaves, slot_no, 1, keepdims=False) - first_leaf
        sibling = jnp.take(tiles, place, axis=0)
        other_coords = sibling[:, :, :feat_cols]
        other_sq = jnp.sum(jnp.square(other_coords.astype(jnp.float32)), axis=-1)
        cross = jnp.einsum(
            "alf,amf->alm", own_coords, other_coords, preferred_element_type=jnp.float32
        )
        block = jnp.exp(-(own_sq[:, :, None] + other_sq[:, None, :] - 2.0 * cross) / spread_width)
        term = jnp.einsum(
            "alm,amr->alr",
            block.astype(jnp.bfloat16),
            sibling[:, :, feat_cols:],
            preferred_element_type=jnp.float32,
        )
        live_rows = (slot_no < near_count)[:, None, None]
        return summed + jnp.where(live_rows, term, 0.0)

    empty = jnp.zeros((leaves_here, leaf_rows, rhs_cols), jnp.float32)
    return lax.fori_loop(0, loop_end, add_slot, empty)


def pair_level(branch, sibling, side_bit, ordering, feat_cols, records, is_top):
    distant = far_term(branch, sibling, feat_cols)
    if is_top:
        records.append((distant, None, None))
        return branch
    paired = jnp.where(
        side_bit == 0,
        jnp.concatenate([branch, sibling], axis=0),
        jnp.concatenate([sibling, branch], axis=0),
    )
    records.append((distant, ordering, side_bit))
    return merge_node(paired, ordering, feat_cols)


def per_device(points, weights, near_leaves, near_count, leaf_perm, local_perm, upper_perm):
    feat_cols = points.shape[1]
    rhs_cols = weights.shape[1]
    leaves_here, leaf_rows = leaf_perm.shape
    skel_rows = leaf_rows // 2
    dev_count = lax.axis_size("dev")
    group_count = lax.axis_size("group")
    devices = dev_count * group_count
    dev_bits = dev_count.bit_length() - 1
    group_bits = group_count.bit_length() - 1
    top_level = dev_bits + group_bits
    local_levels = leaves_here.bit_length() - 1
    dev_index = lax.axis_index("dev")
    group_index = lax.axis_index("group")
    flat_index = group_index * dev_count + dev_index
    stacked = jnp.concatenate([points, weights], axis=1)
    window = with_halo(stacked, (("dev", 0),), stacked.shape[0])
    first_leaf = (dev_index - 1) * leaves_here
    loop_end = near_leaves.shape[1]
    near_part = near_field(
        stacked, window, near_leaves, near_count, feat_cols, first_leaf, loop_end
    )

    def merge_all(stacks, orderings):
        return jax.vmap(lambda one_stack, one_order: merge_node(one_stack, one_order, feat_cols))(
            stacks, orderings
        )

    branches = merge_all(stacked.reshape(leaves_here, leaf_rows, stacked.shape[1]), leaf_perm)
    local_fars = []
    local_orders = []
    for tree_level in range(local_levels):
        node_count = branches.shape[0]
        partner = branches.reshape(node_count // 2, 2, skel_rows, branches.shape[2])[:, ::-1]
        far_partner = partner.reshape(branches.shape)
        local_fars.append(
            jax.vmap(lambda own_rows, sibling: far_term(own_rows, sibling, feat_cols))(
                branches, far_partner
            )
        )
        first_row = leaves_here - leaves_here // 2**tree_level
        ordering = local_perm[0, first_row : first_row + leaves_here // 2 ** (tree_level + 1)]
        local_orders.append(ordering)
        branches = merge_all(
            branches.reshape(node_count // 2, 2 * skel_rows, branches.shape[2]), ordering
        )
    branch = branches[0]
    records = []
    for height in range(dev_bits):
        sibling = swapped(branch, "dev", height)
        side_bit = dev_index >> height & 1
        first_row = devices - devices // 2**height + (flat_index >> height + 1)
        ordering = lax.dynamic_index_in_dim(upper_perm, first_row, 0, keepdims=False)
        branch = pair_level(
            branch, sibling, side_bit, ordering, feat_cols, records, height + 1 == top_level
        )
    for height in range(group_bits):
        tree_level = dev_bits + height
        sibling = swapped(branch, "group", height)
        side_bit = group_index >> height & 1
        first_row = devices - devices // 2**tree_level + (flat_index >> tree_level + 1)
        ordering = lax.dynamic_index_in_dim(
            upper_perm, jnp.minimum(first_row, devices - 3), 0, keepdims=False
        )
        branch = pair_level(
            branch, sibling, side_bit, ordering, feat_cols, records, tree_level + 1 == top_level
        )
    descent = records[-1][0]
    for distant, ordering, side_bit in reversed(records[:-1]):
        spread = expand(descent, ordering)
        descent = distant + merge_gain * lax.dynamic_slice_in_dim(
            spread, side_bit * skel_rows, skel_rows, 0
        )
    descent = descent[None]
    for tree_level in reversed(range(local_levels)):
        spread = jax.vmap(expand)(descent, local_orders[tree_level])
        descent = local_fars[tree_level] + merge_gain * spread.reshape(local_fars[tree_level].shape)
    result = near_part + merge_gain * jax.vmap(expand)(descent, leaf_perm)
    return result.reshape(-1, rhs_cols)


def solution(mesh):
    in_specs = (
        P(("group", "dev"), None),
        P(("group", "dev"), None),
        P(("group", "dev"), None),
        P(("group", "dev")),
        P(("group", "dev"), None),
        P(("group", "dev"), None, None),
        P(),
    )
    out_specs = P(("group", "dev"), None)
    return jax.shard_map(
        per_device, mesh=mesh, in_specs=in_specs, out_specs=out_specs, check_vma=False
    )
```

profile of v0, /device:TPU:0, one launch (start us, length us, event | category | flops | bytes accessed | tf_op | source)
XLA Modules:
  0.0 117.8 jit_solution(8992671306658206055)
XLA Ops:
  0.0 1.5 %copy.11 = bf16[4096,64]{1,0:T(8,128)(2,1)S(1)} copy(bf16[4096,64]{0,1:T(8,128)(2,1)} %param.9) | data formatting | bytes 1048576 | tf_op args[0]
  1.5 1.5 %copy.12 = bf16[4096,64]{1,0:T(8,128)(2,1)S(1)} copy(bf16[4096,64]{0,1:T(8,128)(2,1)} %param.10) | data formatting | bytes 1048576 | tf_op args[1]
  3.1 1.6 %pad_maximum_fusion.1 = bf16[4096,128]{1,0:T(8,128)(2,1)} fusion(bf16[4096,64]{1,0:T(8,128)(2,1)S(1)} %copy.12, bf16[4096,64]{1,0:T(8,128)(2,1)S(1)} %copy.11), kind=kLoop, calls=%fused_computation.125 | loop fusion | flops 2097152 | bytes 2097152 | tf_op jit(solution)/shard_map/concatenate | solution.py:137
  4.6 3.4 %collective-permute-start = (bf16[4096,128]{1,0:T(8,128)(2,1)}, bf16[4096,128]{1,0:T(8,128)(2,1)}, u32[]{:S(2)}, u32[]{:S(2)}) collective-permute-start(bf16[4096,128]{1,0:T(8,128)(2,1)} %pad_maximum_fusion.1), channel_id=1, source_target_pairs={{0,1},{1,2},{2,3},{3,4},{4,5},{5,6},{6,7},{8,9},{9,10},{10,11},{11... | collective-permute-start | bytes 3145736 | tf_op jit(solution)/shard_map/ppermute | solution.py:15
  8.0 1.3 %collective-permute-start.1 = (bf16[4096,128]{1,0:T(8,128)(2,1)}, bf16[4096,128]{1,0:T(8,128)(2,1)}, u32[]{:S(2)}, u32[]{:S(2)}) collective-permute-start(bf16[4096,128]{1,0:T(8,128)(2,1)} %pad_maximum_fusion.1), channel_id=1, source_target_pairs={{1,0},{2,1},{3,2},{4,3},{5,4},{6,5},{7,6},{9,8},{10,9},{11,10},{12... | collective-permute-start | bytes 3145736 | tf_op jit(solution)/shard_map/ppermute | solution.py:18
  9.4 3.0 %multiply_reduce_fusion.3 = (f32[8,256]{1,0:T(8,128)}, bf16[8,256,64]{1,2,0:T(8,128)(2,1)S(1)}) fusion(bf16[8,512,128]{2,1,0:T(8,128)(2,1)} %bitcast, s32[8,256]{1,0:T(8,128)S(1)} %get-tuple-element.216), kind=kOutput, calls=%fused_computation.172 | convolution fusion | flops 135788544 | bytes 1327104 | tf_op jit(solution)/shard_map/vmap()/dot_general | solution.py:55
  12.3 3.3 %fusion.57 = bf16[8,256,64]{1,2,0:T(8,128)(2,1)S(1)} fusion(s32[8,256]{1,0:T(8,128)S(1)} %get-tuple-element.217, s32[8,256]{1,0:T(8,128)S(1)} %get-tuple-element.216, bf16[8,512,128]{2,1,0:T(8,128)(2,1)} %bitcast), kind=kOutput, calls=%fused_computation.56 | convolution fusion | flops 137625600 | bytes 1327104 | tf_op jit(solution)/shard_map/vmap()/dot_general | solution.py:56
  16.0 1.2 %multiply_reduce_fusion.5 = (f32[4,256]{1,0:T(4,128)}, bf16[4,256,64]{1,2,0:T(8,128)(2,1)S(1)}) fusion(bf16[4,512,128]{2,1,0:T(8,128)(2,1)S(1)} %bitcast.105, s32[4,256]{1,0:T(4,128)S(1)} %get-tuple-element.218), kind=kOutput, calls=%fused_computation.219 | convolution fusion | flops 67894272 | bytes 663552 | tf_op jit(solution)/shard_map/vmap()/dot_general | solution.py:55
  17.3 1.3 %fusion.89 = bf16[4,256,64]{1,2,0:T(8,128)(2,1)S(1)} fusion(s32[4,256]{1,0:T(4,128)S(1)} %get-tuple-element.219, s32[4,256]{1,0:T(4,128)S(1)} %get-tuple-element.218, bf16[4,512,128]{2,1,0:T(8,128)(2,1)S(1)} %bitcast.106), kind=kOutput, calls=%fused_computation.90 | convolution fusion | flops 68812800 | bytes 663552 | tf_op jit(solution)/shard_map/vmap()/dot_general | solution.py:56
  19.3 0.7 fusion.99
  20.9 2.3 %collective-permute-start.2 = (bf16[256,128]{0,1:T(8,128)(2,1)S(1)}, bf16[256,128]{0,1:T(8,128)(2,1)S(1)}, u32[]{:S(2)}, u32[]{:S(2)}) collective-permute-start(bf16[256,128]{0,1:T(8,128)(2,1)S(1)} %maximum_bitcast_fusion), channel_id=1, source_target_pairs={{0,1},{1,0},{2,3},{3,2},{4,5},{5,4},{6,7},{7,6},{8,9},{9,8},{10,11... | collective-permute-start | bytes 196616 | tf_op jit(solution)/shard_map/ppermute | solution.py:30
  23.1 0.6 multiply_reduce_fusion.17
  24.1 0.9 fusion.267
  25.0 0.6 multiply_reduce_fusion.4
  25.7 0.7 multiply_reduce_fusion.2
  26.3 1.5 %copy.32 = bf16[8,512,64]{1,2,0:T(8,128)(2,1)S(1)} copy(bf16[8,512,64]{2,1,0:T(8,128)(2,1)} %bitcast.89) | data formatting | bytes 1048576
  28.0 2.2 %fusion.45 = f32[4,256,64]{1,2,0:T(8,128)} fusion(bf16[4,256,64]{1,2,0:T(8,128)(2,1)} %copy-done.4, f32[4,256]{1,0:T(4,128)} %multiply_reduce_fusion.4, f32[4,256]{1,0:T(4,128)} %get-tuple-element.232, bf16[4,256,128]{1,2,0:T(8,128)(2,1)S(1)} %bitcast.104), kind=kOutput, calls=%fused_computation.47 | convolution fusion | flops 68681728 | bytes 663552 | tf_op jit(solution)/shard_map/vmap()/dot_general | solution.py:63
  30.3 2.7 %fusion.36 = f32[8,256,64]{1,2,0:T(8,128)} fusion(bf16[8,256,64]{1,2,0:T(8,128)(2,1)} %copy-done.2, f32[8,256]{1,0:T(8,128)} %multiply_reduce_fusion.2, f32[8,256]{1,0:T(8,128)} %get-tuple-element.234, bf16[8,256,128]{1,2,0:T(8,128)(2,1)S(1)} %bitcast.102), kind=kOutput, calls=%fused_computation.39 | convolution fusion | flops 137363456 | bytes 1327104 | tf_op jit(solution)/shard_map/vmap()/dot_general | solution.py:63
  33.0 0.9 fusion.262
  34.6 1.7 %collective-permute-start.3 = (bf16[256,128]{0,1:T(8,128)(2,1)S(1)}, bf16[256,128]{0,1:T(8,128)(2,1)S(1)}, u32[]{:S(2)}, u32[]{:S(2)}) collective-permute-start(bf16[256,128]{0,1:T(8,128)(2,1)S(1)} %pad_maximum_fusion.5), channel_id=1, source_target_pairs={{0,2},{2,0},{1,3},{3,1},{4,6},{6,4},{5,7},{7,5},{8,10},{10,8},{9,1... | collective-permute-start | bytes 196616 | tf_op jit(solution)/shard_map/ppermute | solution.py:30
  36.4 2.7 %collective-permute-done.3 = bf16[256,128]{0,1:T(8,128)(2,1)S(1)} collective-permute-done((bf16[256,128]{0,1:T(8,128)(2,1)S(1)}, bf16[256,128]{0,1:T(8,128)(2,1)S(1)}, u32[]{:S(2)}, u32[]{:S(2)}) %collective-permute-start.3) | collective-permute-done | bytes 65568 | tf_op jit(solution)/shard_map/ppermute | solution.py:30
  39.8 2.7 %collective-permute-start.4 = (bf16[256,128]{0,1:T(8,128)(2,1)S(1)}, bf16[256,128]{0,1:T(8,128)(2,1)S(1)}, u32[]{:S(2)}, u32[]{:S(2)}) collective-permute-start(bf16[256,128]{0,1:T(8,128)(2,1)S(1)} %pad_maximum_fusion.6), channel_id=1, source_target_pairs={{0,4},{4,0},{1,5},{5,1},{2,6},{6,2},{3,7},{7,3},{8,12},{12,8},{9,1... | collective-permute-start | bytes 196616 | tf_op jit(solution)/shard_map/ppermute | solution.py:30
  42.5 2.2 %collective-permute-done.4 = bf16[256,128]{0,1:T(8,128)(2,1)S(1)} collective-permute-done((bf16[256,128]{0,1:T(8,128)(2,1)S(1)}, bf16[256,128]{0,1:T(8,128)(2,1)S(1)}, u32[]{:S(2)}, u32[]{:S(2)}) %collective-permute-start.4) | collective-permute-done | bytes 65568 | tf_op jit(solution)/shard_map/ppermute | solution.py:30
  45.5 1.6 %collective-permute-start.5 = (bf16[256,128]{0,1:T(8,128)(2,1)S(1)}, bf16[256,128]{0,1:T(8,128)(2,1)S(1)}, u32[]{:S(2)}, u32[]{:S(2)}) collective-permute-start(bf16[256,128]{0,1:T(8,128)(2,1)S(1)} %pad_maximum_fusion.7), channel_id=1, source_target_pairs={{0,8},{8,0},{16,24},{24,16},{1,9},{9,1},{17,25},{25,17},{2,10},{10... | collective-permute-start | bytes 196616 | tf_op jit(solution)/shard_map/ppermute | solution.py:30
  47.1 2.7 %collective-permute-done.5 = bf16[256,128]{0,1:T(8,128)(2,1)S(1)} collective-permute-done((bf16[256,128]{0,1:T(8,128)(2,1)S(1)}, bf16[256,128]{0,1:T(8,128)(2,1)S(1)}, u32[]{:S(2)}, u32[]{:S(2)}) %collective-permute-start.5) | collective-permute-done | bytes 65568 | tf_op jit(solution)/shard_map/ppermute | solution.py:30
  50.5 2.6 %collective-permute-start.6 = (bf16[256,128]{0,1:T(8,128)(2,1)S(1)}, bf16[256,128]{0,1:T(8,128)(2,1)S(1)}, u32[]{:S(2)}, u32[]{:S(2)}) collective-permute-start(bf16[256,128]{0,1:T(8,128)(2,1)S(1)} %pad_maximum_fusion.8), channel_id=1, source_target_pairs={{0,16},{16,0},{8,24},{24,8},{1,17},{17,1},{9,25},{25,9},{2,18},{18... | collective-permute-start | bytes 196616 | tf_op jit(solution)/shard_map/ppermute | solution.py:30
  53.2 2.6 %collective-permute-done.6 = bf16[256,128]{0,1:T(8,128)(2,1)S(1)} collective-permute-done((bf16[256,128]{0,1:T(8,128)(2,1)S(1)}, bf16[256,128]{0,1:T(8,128)(2,1)S(1)}, u32[]{:S(2)}, u32[]{:S(2)}) %collective-permute-start.6) | collective-permute-done | bytes 65568 | tf_op jit(solution)/shard_map/ppermute | solution.py:30
  60.0 0.9 convolution_multiply_fusion.2
  61.7 2.1 %fusion.49 = f32[4,512,64]{1,2,0:T(8,128)S(1)} fusion(s32[4,256]{1,0:T(4,128)S(1)} %copy-done.14, s32[4,256]{1,0:T(4,128)S(1)} %copy-done.12, f32[4,256,64]{1,0,2:T(4,128)S(1)} %copy_add_fusion.1), kind=kOutput, calls=%fused_computation.50 | convolution fusion | flops 404357120 | bytes 794624 | tf_op jit(solution)/shard_map/vmap()/dot_general | solution.py:69
  64.3 1.4 %copy_add_fusion = f32[8,256,64]{1,0,2:T(8,128)S(1)} fusion(f32[8,256,64]{1,0,2:T(8,128)S(1)} %mul.156, f32[8,256,64]{1,2,0:T(8,128)} %fusion.36), kind=kLoop, calls=%fused_computation.144 | loop fusion | flops 131072 | bytes 1572864 | tf_op jit(solution)/shard_map/add | solution.py:198
  65.7 3.5 %fusion.41 = f32[8,512,64]{1,2,0:T(8,128)} fusion(s32[8,256]{1,0:T(8,128)S(1)} %copy-done.10, s32[8,256]{1,0:T(8,128)S(1)} %copy-done.8, f32[8,256,64]{1,0,2:T(8,128)S(1)} %copy_add_fusion), kind=kOutput, calls=%fused_computation.45 | convolution fusion | flops 808714240 | bytes 1589248 | tf_op jit(solution)/shard_map/vmap()/dot_general | solution.py:69
  69.2 12.0 %pad_maximum_fusion = bf16[12288,128]{1,0:T(8,128)(2,1)} fusion(bf16[4096,128]{1,0:T(8,128)(2,1)} %collective-permute-done.1, bf16[4096,64]{1,0:T(8,128)(2,1)S(1)} %copy.12, bf16[4096,64]{1,0:T(8,128)(2,1)S(1)} %copy.11, bf16[4096,128]{1,0:T(8,128)(2,1)} %collective-permute-done), kind=kLoop, calls=%fused_computation.26 | loop fusion | flops 12582912 | bytes 6291456 | tf_op jit(solution)/shard_map/concatenate | solution.py:19
  81.2 34.1 %while.14 = (s32[]{:T(128)}, f32[8,512,64]{1,2,0:T(8,128)S(1)}, s32[8]{0:T(128)S(1)}, f32[8,512]{1,0:T(8,128)S(1)}, s32[8,4]{0,1:T(4,128)}, /*index=5*/s32[]{:T(...) while((s32[]{:T(128)}, f32[8,512,64]{1,2,0:T(8,128)S(1)}, ...), condition=%wide.region_3.4_spmd.clone, body=%wide.region_1.3_spmd.clone.sunk | while | flops 551547968 | bytes 10539323 | solution.py:105
  81.2 0.7 and_bitcast_fusion.2
  81.9 2.6 %gather_fusion = bf16[8,512,128]{2,1,0:T(8,128)(2,1)S(1)} fusion(bf16[24,512,128]{2,1,0:T(8,128)(2,1)} %get-tuple-element.315, s32[1024]{0:T(1024)S(1)} %pad_clamp_fusion.2), kind=kCustom, calls=%fused_computation.clone.clone.1 | custom fusion | bytes 2097184 | tf_op jit(solution)/shard_map/while/body/eval_jaxpr/jit(_take)/gather | solution.py:88
  84.5 0.5 copy.50
  85.4 4.3 %fusion.294 = f32[8,512,64]{1,2,0:T(8,128)S(1)} fusion(f32[8,512]{1,0:T(8,128)S(1)} %multiply_reduce_fusion.19, f32[8,512]{1,0:T(8,128)S(1)} %get-tuple-element.312, bf16[8,512,64]{2,1,0:T(8,128)(2,1)} %get-tuple-element.316, f32[8,512,64]{1,2,0:T(8,128)S(1)} %get-tuple-element.300, bf16[8,512,128]{1,2,0:T(8,128)(2,1)S(1)} %broadcast_select_fusion.2, ...), kind=kOutput, calls=%fused_computation.9.clone.1 | convolution fusion | flops 550240256 | bytes 3702793 | tf_op jit(solution)/shard_map/while/body/eval_jaxpr/alm,amr->alr/dot_general | solution.py:95
  89.7 0.7 and_bitcast_fusion.2
  90.4 2.6 %gather_fusion = bf16[8,512,128]{2,1,0:T(8,128)(2,1)S(1)} fusion(bf16[24,512,128]{2,1,0:T(8,128)(2,1)} %get-tuple-element.315, s32[1024]{0:T(1024)S(1)} %pad_clamp_fusion.2), kind=kCustom, calls=%fused_computation.clone.clone.1 | custom fusion | bytes 2097184 | tf_op jit(solution)/shard_map/while/body/eval_jaxpr/jit(_take)/gather | solution.py:88
  93.9 4.3 %fusion.294 = f32[8,512,64]{1,2,0:T(8,128)S(1)} fusion(f32[8,512]{1,0:T(8,128)S(1)} %multiply_reduce_fusion.19, f32[8,512]{1,0:T(8,128)S(1)} %get-tuple-element.312, bf16[8,512,64]{2,1,0:T(8,128)(2,1)} %get-tuple-element.316, f32[8,512,64]{1,2,0:T(8,128)S(1)} %get-tuple-element.300, bf16[8,512,128]{1,2,0:T(8,128)(2,1)S(1)} %broadcast_select_fusion.2, ...), kind=kOutput, calls=%fused_computation.9.clone.1 | convolution fusion | flops 550240256 | bytes 3702793 | tf_op jit(solution)/shard_map/while/body/eval_jaxpr/alm,amr->alr/dot_general | solution.py:95
  98.2 0.7 and_bitcast_fusion.2
  98.9 2.6 %gather_fusion = bf16[8,512,128]{2,1,0:T(8,128)(2,1)S(1)} fusion(bf16[24,512,128]{2,1,0:T(8,128)(2,1)} %get-tuple-element.315, s32[1024]{0:T(1024)S(1)} %pad_clamp_fusion.2), kind=kCustom, calls=%fused_computation.clone.clone.1 | custom fusion | bytes 2097184 | tf_op jit(solution)/shard_map/while/body/eval_jaxpr/jit(_take)/gather | solution.py:88
  102.4 4.3 %fusion.294 = f32[8,512,64]{1,2,0:T(8,128)S(1)} fusion(f32[8,512]{1,0:T(8,128)S(1)} %multiply_reduce_fusion.19, f32[8,512]{1,0:T(8,128)S(1)} %get-tuple-element.312, bf16[8,512,64]{2,1,0:T(8,128)(2,1)} %get-tuple-element.316, f32[8,512,64]{1,2,0:T(8,128)S(1)} %get-tuple-element.300, bf16[8,512,128]{1,2,0:T(8,128)(2,1)S(1)} %broadcast_select_fusion.2, ...), kind=kOutput, calls=%fused_computation.9.clone.1 | convolution fusion | flops 550240256 | bytes 3702793 | tf_op jit(solution)/shard_map/while/body/eval_jaxpr/alm,amr->alr/dot_general | solution.py:95
  106.7 0.7 and_bitcast_fusion.2
  107.5 2.6 %gather_fusion = bf16[8,512,128]{2,1,0:T(8,128)(2,1)S(1)} fusion(bf16[24,512,128]{2,1,0:T(8,128)(2,1)} %get-tuple-element.315, s32[1024]{0:T(1024)S(1)} %pad_clamp_fusion.2), kind=kCustom, calls=%fused_computation.clone.clone.1 | custom fusion | bytes 2097184 | tf_op jit(solution)/shard_map/while/body/eval_jaxpr/jit(_take)/gather | solution.py:88
  111.0 4.3 %fusion.294 = f32[8,512,64]{1,2,0:T(8,128)S(1)} fusion(f32[8,512]{1,0:T(8,128)S(1)} %multiply_reduce_fusion.19, f32[8,512]{1,0:T(8,128)S(1)} %get-tuple-element.312, bf16[8,512,64]{2,1,0:T(8,128)(2,1)} %get-tuple-element.316, f32[8,512,64]{1,2,0:T(8,128)S(1)} %get-tuple-element.300, bf16[8,512,128]{1,2,0:T(8,128)(2,1)S(1)} %broadcast_select_fusion.2, ...), kind=kOutput, calls=%fused_computation.9.clone.1 | convolution fusion | flops 550240256 | bytes 3702793 | tf_op jit(solution)/shard_map/while/body/eval_jaxpr/alm,amr->alr/dot_general | solution.py:95
  115.3 1.4 %add_bitcast_fusion = f32[8,8,8,512]{3,2,1,0:T(8,128)S(1)} fusion(f32[8,512,64]{1,2,0:T(8,128)S(1)} %get-tuple-element.144, f32[8,512,64]{1,2,0:T(8,128)} %fusion.41), kind=kLoop, calls=%fused_computation.126 | loop fusion | flops 262144 | bytes 3145728
  116.7 1.1 copy.38
  (136 shorter events, 13.4 us)
Async XLA Ops:
  0.0 9.3 %copy-start.5 = (s32[1,7,512]{2,0,1:T(1,128)S(1)}, s32[1,7,512]{2,0,1:T(1,128)}, u32[]{:S(2)}) copy-start(s32[1,7,512]{2,0,1:T(1,128)} %param.14) | copy-start | bytes 43012
  0.0 9.3 %copy-start.6 = (s32[8,512]{1,0:T(8,128)S(1)}, s32[8,512]{1,0:T(8,128)}, u32[]{:S(2)}) copy-start(s32[8,512]{1,0:T(8,128)} %param.13) | copy-start | bytes 49156
  4.6 64.6 %collective-permute-start = (bf16[4096,128]{1,0:T(8,128)(2,1)}, bf16[4096,128]{1,0:T(8,128)(2,1)}, u32[]{:S(2)}, u32[]{:S(2)}) collective-permute-start(bf16[4096,128]{1,0:T(8,128)(2,1)} %pad_maximum_fusion.1), channel_id=1, source_target_pairs={{0,1},{1,2},{2,3},{3,4},{4,5},{5,6},{6,7},{8,9},{9,10},{10,11},{11... | collective-permute-start | bytes 3145736 | tf_op jit(solution)/shard_map/ppermute | solution.py:15
  8.0 61.2 %collective-permute-start.1 = (bf16[4096,128]{1,0:T(8,128)(2,1)}, bf16[4096,128]{1,0:T(8,128)(2,1)}, u32[]{:S(2)}, u32[]{:S(2)}) collective-permute-start(bf16[4096,128]{1,0:T(8,128)(2,1)} %pad_maximum_fusion.1), channel_id=1, source_target_pairs={{1,0},{2,1},{3,2},{4,3},{5,4},{6,5},{7,6},{9,8},{10,9},{11,10},{12... | collective-permute-start | bytes 3145736 | tf_op jit(solution)/shard_map/ppermute | solution.py:18
  9.3 6.3 %copy-start.7 = (s32[8,256]{1,0:T(8,128)}, s32[8,256]{1,0:T(8,128)S(1)}, u32[]{:S(2)}) copy-start(s32[8,256]{1,0:T(8,128)S(1)} %get-tuple-element.216) | copy-start | bytes 24580
  9.3 6.3 %copy-start.9 = (s32[8,256]{1,0:T(8,128)}, s32[8,256]{1,0:T(8,128)S(1)}, u32[]{:S(2)}) copy-start(s32[8,256]{1,0:T(8,128)S(1)} %get-tuple-element.217) | copy-start | bytes 24580
  12.3 3.3 %copy-start.2 = (bf16[8,256,64]{1,2,0:T(8,128)(2,1)}, bf16[8,256,64]{1,2,0:T(8,128)(2,1)S(1)}, u32[]{:S(2)}) copy-start(bf16[8,256,64]{1,2,0:T(8,128)(2,1)S(1)} %get-tuple-element.235) | copy-start | bytes 786436
  12.3 3.7 %slice-start = ((s32[1,7,512]{2,0,1:T(1,128)}), s32[1,4,512]{2,0,1:T(1,128)S(1)}, s32[]{:S(2)}) async-start(s32[1,7,512]{2,0,1:T(1,128)} %param.14), calls=%async_computation | async-start | bytes 16384 | tf_op jit(solution)/shard_map/slice | solution.py:163
  15.7 3.1 %slice-start.1 = ((s32[1,7,512]{2,0,1:T(1,128)}), s32[1,2,512]{2,0,1:T(1,128)S(1)}, s32[]{:S(2)}) async-start(s32[1,7,512]{2,0,1:T(1,128)} %param.14), calls=%async_computation.1 | async-start | bytes 8192 | tf_op jit(solution)/shard_map/slice | solution.py:163
  16.0 2.6 %copy-start.11 = (s32[4,256]{1,0:T(4,128)}, s32[4,256]{1,0:T(4,128)S(1)}, u32[]{:S(2)}) copy-start(s32[4,256]{1,0:T(4,128)S(1)} %get-tuple-element.218) | copy-start | bytes 12292
  16.0 3.3 %copy-start.13 = (s32[4,256]{1,0:T(4,128)}, s32[4,256]{1,0:T(4,128)S(1)}, u32[]{:S(2)}) copy-start(s32[4,256]{1,0:T(4,128)S(1)} %get-tuple-element.219) | copy-start | bytes 12292
  17.3 1.3 %copy-start.4 = (bf16[4,256,64]{1,2,0:T(8,128)(2,1)}, bf16[4,256,64]{1,2,0:T(8,128)(2,1)S(1)}, u32[]{:S(2)}) copy-start(bf16[4,256,64]{1,2,0:T(8,128)(2,1)S(1)} %get-tuple-element.233) | copy-start | bytes 393220
  18.9 1.1 copy-start.15
  18.9 1.1 copy-start.17
  20.2 3.6 %copy-start.20 = (s32[1,256]{1,0:T(1,128)}, s32[1,256]{1,0:T(1,128)S(1)}, u32[]{:S(2)}) copy-start(s32[1,256]{1,0:T(1,128)S(1)} %get-tuple-element.222) | copy-start | bytes 3076
  20.2 3.6 %copy-start.22 = (s32[1,256]{1,0:T(1,128)}, s32[1,256]{1,0:T(1,128)S(1)}, u32[]{:S(2)}) copy-start(s32[1,256]{1,0:T(1,128)S(1)} %get-tuple-element.223) | copy-start | bytes 3076
  20.9 13.0 %collective-permute-start.2 = (bf16[256,128]{0,1:T(8,128)(2,1)S(1)}, bf16[256,128]{0,1:T(8,128)(2,1)S(1)}, u32[]{:S(2)}, u32[]{:S(2)}) collective-permute-start(bf16[256,128]{0,1:T(8,128)(2,1)S(1)} %maximum_bitcast_fusion), channel_id=1, source_target_pairs={{0,1},{1,0},{2,3},{3,2},{4,5},{5,4},{6,7},{7,6},{8,9},{9,8},{10,11... | collective-permute-start | bytes 196616 | tf_op jit(solution)/shard_map/ppermute | solution.py:30
  34.6 4.4 %collective-permute-start.3 = (bf16[256,128]{0,1:T(8,128)(2,1)S(1)}, bf16[256,128]{0,1:T(8,128)(2,1)S(1)}, u32[]{:S(2)}, u32[]{:S(2)}) collective-permute-start(bf16[256,128]{0,1:T(8,128)(2,1)S(1)} %pad_maximum_fusion.5), channel_id=1, source_target_pairs={{0,2},{2,0},{1,3},{3,1},{4,6},{6,4},{5,7},{7,5},{8,10},{10,8},{9,1... | collective-permute-start | bytes 196616 | tf_op jit(solution)/shard_map/ppermute | solution.py:30
  39.8 5.0 %collective-permute-start.4 = (bf16[256,128]{0,1:T(8,128)(2,1)S(1)}, bf16[256,128]{0,1:T(8,128)(2,1)S(1)}, u32[]{:S(2)}, u32[]{:S(2)}) collective-permute-start(bf16[256,128]{0,1:T(8,128)(2,1)S(1)} %pad_maximum_fusion.6), channel_id=1, source_target_pairs={{0,4},{4,0},{1,5},{5,1},{2,6},{6,2},{3,7},{7,3},{8,12},{12,8},{9,1... | collective-permute-start | bytes 196616 | tf_op jit(solution)/shard_map/ppermute | solution.py:30
  45.1 14.0 %copy-start.19 = (f32[256]{0:T(256)S(1)}, f32[256]{0:T(256)}, u32[]{:S(2)}) copy-start(f32[256]{0:T(256)} %multiply_reduce_fusion.17) | copy-start | bytes 3076
  45.4 14.1 %copy-start.3 = (f32[2,256,64]{1,2,0:T(8,128)S(1)}, f32[2,256,64]{1,2,0:T(8,128)}, u32[]{:S(2)}) copy-start(f32[2,256,64]{1,2,0:T(8,128)} %fusion.267) | copy-start | bytes 393220
  45.5 14.1 %copy-start.21 = (s32[1,256]{1,0:T(1,128)S(1)}, s32[1,256]{1,0:T(1,128)}, u32[]{:S(2)}) copy-start(s32[1,256]{1,0:T(1,128)} %copy-done.20) | copy-start | bytes 3076
  45.5 14.1 %copy-start.23 = (s32[1,256]{1,0:T(1,128)S(1)}, s32[1,256]{1,0:T(1,128)}, u32[]{:S(2)}) copy-start(s32[1,256]{1,0:T(1,128)} %copy-done.22) | copy-start | bytes 3076
  45.5 4.3 %collective-permute-start.5 = (bf16[256,128]{0,1:T(8,128)(2,1)S(1)}, bf16[256,128]{0,1:T(8,128)(2,1)S(1)}, u32[]{:S(2)}, u32[]{:S(2)}) collective-permute-start(bf16[256,128]{0,1:T(8,128)(2,1)S(1)} %pad_maximum_fusion.7), channel_id=1, source_target_pairs={{0,8},{8,0},{16,24},{24,16},{1,9},{9,1},{17,25},{25,17},{2,10},{10... | collective-permute-start | bytes 196616 | tf_op jit(solution)/shard_map/ppermute | solution.py:30
  49.9 10.2 %copy-start.16 = (s32[2,256]{1,0:T(2,128)S(1)}, s32[2,256]{1,0:T(2,128)}, u32[]{:S(2)}) copy-start(s32[2,256]{1,0:T(2,128)} %copy-done.15) | copy-start | bytes 6148
  49.9 10.2 %copy-start.18 = (s32[2,256]{1,0:T(2,128)S(1)}, s32[2,256]{1,0:T(2,128)}, u32[]{:S(2)}) copy-start(s32[2,256]{1,0:T(2,128)} %copy-done.17) | copy-start | bytes 6148
  50.5 5.2 %collective-permute-start.6 = (bf16[256,128]{0,1:T(8,128)(2,1)S(1)}, bf16[256,128]{0,1:T(8,128)(2,1)S(1)}, u32[]{:S(2)}, u32[]{:S(2)}) collective-permute-start(bf16[256,128]{0,1:T(8,128)(2,1)S(1)} %pad_maximum_fusion.8), channel_id=1, source_target_pairs={{0,16},{16,0},{8,24},{24,8},{1,17},{17,1},{9,25},{25,9},{2,18},{18... | collective-permute-start | bytes 196616 | tf_op jit(solution)/shard_map/ppermute | solution.py:30
  56.6 4.8 %copy-start.1 = (f32[4,256,64]{1,2,0:T(8,128)S(1)}, f32[4,256,64]{1,2,0:T(8,128)}, u32[]{:S(2)}) copy-start(f32[4,256,64]{1,2,0:T(8,128)} %fusion.45) | copy-start | bytes 786436
  57.0 4.7 %copy-start.12 = (s32[4,256]{1,0:T(4,128)S(1)}, s32[4,256]{1,0:T(4,128)}, u32[]{:S(2)}) copy-start(s32[4,256]{1,0:T(4,128)} %copy-done.11) | copy-start | bytes 12292
  57.0 4.7 %copy-start.14 = (s32[4,256]{1,0:T(4,128)S(1)}, s32[4,256]{1,0:T(4,128)}, u32[]{:S(2)}) copy-start(s32[4,256]{1,0:T(4,128)} %copy-done.13) | copy-start | bytes 12292
  61.7 4.0 %copy-start.8 = (s32[8,256]{1,0:T(8,128)S(1)}, s32[8,256]{1,0:T(8,128)}, u32[]{:S(2)}) copy-start(s32[8,256]{1,0:T(8,128)} %copy-done.7) | copy-start | bytes 24580
  61.7 4.0 %copy-start.10 = (s32[8,256]{1,0:T(8,128)S(1)}, s32[8,256]{1,0:T(8,128)}, u32[]{:S(2)}) copy-start(s32[8,256]{1,0:T(8,128)} %copy-done.9) | copy-start | bytes 24580
  69.2 12.0 %copy-start = (f32[8,512,64]{1,2,0:T(8,128)S(1)}, f32[8,512,64]{1,2,0:T(8,128)}, u32[]{:S(2)}) copy-start(f32[8,512,64]{1,2,0:T(8,128)} %custom-call) | copy-start | bytes 3145732
  69.2 12.0 %copy-start.24 = (s32[8]{0:T(128)S(1)}, s32[8]{0:T(128)}, u32[]{:S(2)}) copy-start(s32[8]{0:T(128)} %param.12) | copy-start | bytes 100
where the time goes:
time: 119 us; the launch traced here: 118 us
  matrix products  47 us (39%)
  other arithmetic  23 us (19%)
  local copies, waits for them, and re-layouts  21 us (18%)
  starting transfers between devices  15.7 us (13%)
  waiting for transfers between devices  10.2 us (9%)
    dot_general x4, matrix products, add_slot(): jnp.einsum('alm,amr->alr', block.astype(jnp.bfloat16), sibling[:, :, feat...  17.1 us
    gather x8, local copies, waits for them, and re-layouts, add_slot(): sibling = jnp.take(tiles, place, axis=0)  12.7 us
    concatenate x1, other arithmetic, with_halo(): block = jnp.concatenate([low, block, high], axis=dim)  12 us
    ppermute x5, starting transfers between devices, swapped(): return lax.ppermute(block, axis, route)  11 us
    ppermute x5, waiting for transfers between devices, swapped(): return lax.ppermute(block, axis, route)  10.2 us
    dot_general x8, matrix products, expand(): lax.dot_general(both_table, values, (((0,), (0,)), ((), ())), precision=l...  8.7 us
    dot_general x8, matrix products, far_term(): jnp.dot(block, sibling[:, feat_cols:], preferred_element_type=jnp.float32)  7.64 us
    dot_general x8, matrix products, merge_node(): jnp.dot(both_table, stacked[:, feat_cols:], preferred_element_type=jnp.fl...  7.02 us
  transfers between devices with their start and end apart: 7, of which 4 were waited for; matrix products, arithmetic and copies ran while one was open for 32% of the time, Pallas kernels for 0%

commit v1 on v0

v1 whole, which is shorter than its diff:
```python
import functools
import math

import jax
import jax.numpy as jnp
from jax import lax
from jax.experimental import pallas as pl
from jax.experimental.pallas import tpu as pltpu
from jax.sharding import PartitionSpec as P

spread_width = 10.0
merge_gain = 0.8408964152537145
exp2_scale = 2.0 / spread_width * math.log2(math.e)
bf16 = jnp.bfloat16
f32 = jnp.float32


def half_squares(coords):
    wide = coords.astype(f32)
    total = -0.5 * jnp.sum(wide * wide, axis=0, keepdims=True)
    high = total.astype(bf16).astype(f32)
    rest = total - high
    mid = rest.astype(bf16).astype(f32)
    return high, mid, rest - mid


def with_squares(coords, squares_first):
    high, mid, low = half_squares(coords)
    shape = (16, coords.shape[1])
    row = lax.broadcasted_iota(jnp.int32, shape, 0)
    at = 0 if squares_first else 3
    ones = (row >= 3 - at) & (row < 6 - at)
    extra = jnp.where(ones, 1.0, 0.0)
    for offset, part in enumerate((high, mid, low)):
        extra = jnp.where(row == at + offset, jnp.broadcast_to(part, shape), extra)
    return jnp.concatenate([coords, extra.astype(bf16)], axis=0)


def kernel_block(source, target):
    inner = lax.dot_general(source, target, (((0,), (0,)), ((), ())), preferred_element_type=f32)
    return jnp.exp2(inner * exp2_scale).astype(bf16)


def apply(rhs, block):
    return jnp.dot(rhs, block, preferred_element_type=f32)


def apply_flipped(rhs, block):
    return lax.dot_general(rhs, block, (((1,), (1,)), ((), ())), preferred_element_type=f32)


def tables(order, head_ref, both_ref, at):
    size = order.shape[1]
    half = size // 2
    row = lax.broadcasted_iota(jnp.int32, (size, half), 0)
    head = order[:, :half] == row
    tail = order[:, half:] == row
    head_ref[at] = jnp.where(head, 1.0, 0.0).astype(bf16)
    both_ref[at] = jnp.where(head | tail, 1.0, 0.0).astype(bf16)


def merge(coords, rhs, head, both):
    picked = jnp.dot(coords, head, preferred_element_type=f32).astype(bf16)
    summed = merge_gain * jnp.dot(rhs, both, preferred_element_type=f32)
    return jnp.concatenate([picked, summed.astype(bf16)], axis=0)


def expand(values, both):
    high = values.astype(bf16)
    low = (values - high.astype(f32)).astype(bf16)
    spread = apply_flipped(jnp.concatenate([high, low], axis=0), both)
    rows = values.shape[0]
    return spread[:rows] + spread[rows:]


def tree_kernel(
    leaves,
    leaf_rows,
    feat,
    dev_count,
    group_count,
    p_ref,
    w_ref,
    leaf_ref,
    local_ref,
    upper_ref,
    part_ref,
    winp_ref,
    winw_ref,
    stack,
    head_t,
    both_t,
    far,
    down,
    send_sem,
    recv_sem,
    halo_send,
    halo_recv,
    own_sem,
):
    skel = leaf_rows // 2
    devices = dev_count * group_count
    dev_bits = dev_count.bit_length() - 1
    group_bits = group_count.bit_length() - 1
    rounds = dev_bits + group_bits
    local_levels = leaves.bit_length() - 1
    dev = lax.axis_index("dev")
    group = lax.axis_index("group")
    flat = group * dev_count + dev

    def partner(height):
        if height < dev_bits:
            side = dev // 2**height % 2
            return {"dev": dev + (1 - 2 * side) * 2**height}, side
        stride = 2 ** (height - dev_bits)
        side = group // stride % 2
        return {"group": group + (1 - 2 * side) * stride}, side

    barrier = pltpu.get_barrier_semaphore()
    for height in range(rounds):
        pl.semaphore_signal(
            barrier, inc=1, device_id=partner(height)[0], device_id_type=pl.DeviceIdType.MESH
        )

    beside = dev + 2 * lax.rem(dev, 2) - 1
    has_beside = (beside >= 0) & (beside < dev_count)

    @pl.when(has_beside)
    def _():
        pl.semaphore_signal(
            barrier, inc=1, device_id={"dev": beside}, device_id_type=pl.DeviceIdType.MESH
        )

    pl.semaphore_wait(barrier, rounds + has_beside.astype(jnp.int32))

    def halo(to_right):
        other = lax.rem(dev + 1, dev_count) if to_right else lax.rem(dev + dev_count - 1, dev_count)
        slot = 0 if to_right else 2
        row = 1 if to_right else 0
        return [
            pltpu.make_async_remote_copy(
                src_ref=src,
                dst_ref=dst.at[slot],
                send_sem=halo_send.at[row, k],
                recv_sem=halo_recv.at[row, k],
                device_id={"dev": other},
                device_id_type=pl.DeviceIdType.MESH,
            )
            for k, (src, dst) in enumerate(((p_ref, winp_ref), (w_ref, winw_ref)))
        ]

    def start(copies):
        for copy in copies:
            copy.start()

    pl.when(dev > 0)(lambda: start(halo(False)))
    pl.when(dev < dev_count - 1)(lambda: start(halo(True)))
    own_copies = [
        pltpu.make_async_copy(p_ref, winp_ref.at[1], own_sem.at[0]),
        pltpu.make_async_copy(w_ref, winw_ref.at[1], own_sem.at[1]),
    ]
    start(own_copies)

    def leaf_cols(leaf):
        return pl.ds(pl.multiple_of(leaf * leaf_rows, leaf_rows), leaf_rows)

    pair_base = [leaves - leaves // 2**t for t in range(local_levels)]
    top_pair = leaves - 1
    node_base = [2 * base for base in pair_base]
    top_node = 2 * top_pair
    table_base = [0] + [leaves + base for base in pair_base]
    top_table = 2 * leaves - 1

    def up_leaves(pair, carry):
        for k in range(2):
            leaf = 2 * pair + k
            tables(leaf_ref[pl.ds(leaf, 1), :], head_t, both_t, leaf)
            cols = leaf_cols(leaf)
            stack[pair, k] = merge(p_ref[:, cols], w_ref[:, cols], head_t[leaf], both_t[leaf])
        return carry

    lax.fori_loop(0, leaves // 2, up_leaves, 0)

    def merge_pair(pair, table):
        two = jnp.concatenate([stack[pair, 0], stack[pair, 1]], axis=1)
        return merge(two[:feat], two[feat:], head_t[table], both_t[table])

    side0 = partner(0)[1]
    for t in range(local_levels):
        count = leaves // 2 ** (t + 1)
        for i in range(count):
            row = pair_base[t] + i
            tables(local_ref[row : row + 1, :], head_t, both_t, table_base[t + 1] + i)
            merged = merge_pair(pair_base[t] + i, table_base[t + 1] + i)
            if t + 1 < local_levels:
                stack[pair_base[t + 1] + i // 2, i % 2] = merged
            else:
                stack[top_pair, side0] = merged

    def local_far(pair, carry):
        first, second = stack[pair, 0], stack[pair, 1]
        block = kernel_block(with_squares(first[:feat], True), with_squares(second[:feat], False))
        far[2 * pair + 1] = apply(first[feat:], block)
        far[2 * pair] = apply_flipped(second[feat:], block)
        return carry

    def near_own(leaf, carry):
        cols = leaf_cols(leaf)
        coords = p_ref[:, cols]
        block = kernel_block(with_squares(coords, True), with_squares(coords, False))
        part_ref[:, cols] = apply(w_ref[:, cols], block)
        return carry

    def cross_far(height):
        side = partner(height)[1]
        own = stack[top_pair + height, side]
        other = stack[top_pair + height, 1 - side]
        block = kernel_block(with_squares(other[:feat], True), with_squares(own[:feat], False))
        far[top_node + height] = apply(other[feat:], block)

    def exchange(height):
        target, side = partner(height)
        return pltpu.make_async_remote_copy(
            src_ref=stack.at[top_pair + height, side],
            dst_ref=stack.at[top_pair + height, side],
            send_sem=send_sem.at[height],
            recv_sem=recv_sem.at[height],
            device_id=target,
            device_id_type=pl.DeviceIdType.MESH,
        )

    shares = max(rounds - 1, 1)
    bounds = [leaves * k // shares for k in range(shares + 1)]
    copies = []
    for height in range(rounds):
        copy = exchange(height)
        copy.start()
        copies.append(copy)
        if height == 0:
            for level in range(rounds - 1):
                row = devices - devices // 2**level + flat // 2 ** (level + 1)
                tables(upper_ref[pl.ds(row, 1), :], head_t, both_t, top_table + level)
            lax.fori_loop(0, leaves - 1, local_far, 0)
        else:
            cross_far(height - 1)
            if bounds[height] > bounds[height - 1]:
                lax.fori_loop(bounds[height - 1], bounds[height], near_own, 0)
        copy.wait_recv()
        if height + 1 < rounds:
            stack[top_pair + height + 1, partner(height + 1)[1]] = merge_pair(
                top_pair + height, top_table + height
            )
    cross_far(rounds - 1)
    if rounds == 1:
        lax.fori_loop(0, leaves, near_own, 0)

    descent = far[top_node + rounds - 1]
    for height in range(rounds - 2, -1, -1):
        rows = pl.ds(pl.multiple_of(partner(height + 0)[1] * skel, skel), skel)
        spread = expand(descent, both_t[top_table + height, rows, :])
        descent = far[top_node + height] + merge_gain * spread
    down[0] = descent
    for t in range(local_levels - 1, -1, -1):
        count = leaves // 2 ** (t + 1)
        values = [down[i] for i in range(count)]
        for i in range(count):
            spread = expand(values[i], both_t[table_base[t + 1] + i])
            node = node_base[t] + 2 * i
            down[2 * i] = far[node] + merge_gain * spread[:, :skel]
            down[2 * i + 1] = far[node + 1] + merge_gain * spread[:, skel:]

    def last(pair, carry):
        for k in range(2):
            leaf = 2 * pair + k
            part_ref[:, leaf_cols(leaf)] += merge_gain * expand(down[leaf], both_t[leaf])
        return carry

    lax.fori_loop(0, leaves // 2, last, 0)

    for copy in copies:
        copy.wait_send()

    def finish(sent, received):
        for copy in sent:
            copy.wait_send()
        for copy in received:
            copy.wait_recv()

    pl.when(dev > 0)(lambda: finish(halo(False), halo(True)))
    pl.when(dev < dev_count - 1)(lambda: finish(halo(True), halo(False)))
    for copy in own_copies:
        copy.wait()


def near_kernel(leaves, leaf_rows, near_ref, count_ref, part_ref, winp_ref, winw_ref, out_ref):
    first_leaf = (lax.axis_index("dev") - 1) * leaves

    def one_leaf(leaf, carry):
        cols = pl.ds(pl.multiple_of(leaf * leaf_rows, leaf_rows), leaf_rows)
        out_ref[:, cols] = part_ref[:, cols]
        target = with_squares(winp_ref[1, :, cols], False)

        def one_slot(slot, inner):
            place = near_ref[leaf, slot] - first_leaf
            side = place // leaves
            other = pl.ds(pl.multiple_of((place - side * leaves) * leaf_rows, leaf_rows), leaf_rows)
            block = kernel_block(with_squares(winp_ref[side, :, other], True), target)
            out_ref[:, cols] += apply(winw_ref[side, :, other], block)
            return inner

        lax.fori_loop(1, count_ref[leaf], one_slot, 0)
        return carry

    lax.fori_loop(0, leaves, one_leaf, 0)


def per_device(
    dev_count, group_count, points, weights, near_leaves, near_count, leaf_perm, local_perm, upper_perm
):
    feat = points.shape[1]
    rhs = weights.shape[1]
    rows = points.shape[0]
    leaves, leaf_rows = leaf_perm.shape
    skel = leaf_rows // 2
    rounds = (dev_count * group_count).bit_length() - 1
    vmem = pl.BlockSpec(memory_space=pltpu.VMEM)
    smem = pl.BlockSpec(memory_space=pltpu.SMEM)
    hbm = pl.BlockSpec(memory_space=pl.ANY)
    part, win_p, win_w = pl.pallas_call(
        functools.partial(tree_kernel, leaves, leaf_rows, feat, dev_count, group_count),
        out_shape=[
            jax.ShapeDtypeStruct((rhs, rows), f32),
            jax.ShapeDtypeStruct((3, feat, rows), bf16),
            jax.ShapeDtypeStruct((3, rhs, rows), bf16),
        ],
        in_specs=[vmem] * 5,
        out_specs=[vmem, hbm, hbm],
        scratch_shapes=[
            pltpu.VMEM((leaves - 1 + rounds, 2, feat + rhs, skel), bf16),
            pltpu.VMEM((2 * leaves - 2 + rounds, leaf_rows, skel), bf16),
            pltpu.VMEM((2 * leaves - 2 + rounds, leaf_rows, skel), bf16),
            pltpu.VMEM((2 * leaves - 2 + rounds, rhs, skel), f32),
            pltpu.VMEM((leaves, rhs, skel), f32),
            pltpu.SemaphoreType.DMA((rounds,)),
            pltpu.SemaphoreType.DMA((rounds,)),
            pltpu.SemaphoreType.DMA((2, 2)),
            pltpu.SemaphoreType.DMA((2, 2)),
            pltpu.SemaphoreType.DMA((2,)),
        ],
        compiler_params=pltpu.CompilerParams(
            collective_id=0, has_side_effects=True, vmem_limit_bytes=48 * 2**20
        ),
        name="tree",
    )(points.T, weights.T, leaf_perm, local_perm[0], upper_perm)
    product = pl.pallas_call(
        functools.partial(near_kernel, leaves, leaf_rows),
        out_shape=jax.ShapeDtypeStruct((rhs, rows), f32),
        in_specs=[smem, smem, vmem, vmem, vmem],
        out_specs=vmem,
        compiler_params=pltpu.CompilerParams(vmem_limit_bytes=48 * 2**20),
        name="near",
    )(near_leaves, near_count, part, win_p, win_w)
    return product.T


def solution(mesh):
    sizes = dict(mesh.shape)
    both = ("group", "dev")
    in_specs = (
        P(both, None),
        P(both, None),
        P(both, None),
        P(both),
        P(both, None),
        P(both, None, None),
        P(),
    )
    return jax.shard_map(
        functools.partial(per_device, sizes["dev"], sizes["group"]),
        mesh=mesh,
        in_specs=in_specs,
        out_specs=P(both, None),
        check_vma=False,
    )
```

time: 119 us -> 56.7 us (0.48)
  the two profiles are of different devices: /device:TPU:0 before, /device:TPU:2 now
where the time goes in v1:
time: 56.7 us; the launch traced here: 55.8 us
  Pallas kernels  50 us (88%)
  local copies, waits for them, and re-layouts  5.76 us (10%)
    pallas_call x1, Pallas kernels, per_device(): pl.pallas_call(functools.partial(tree_kernel, leaves, leaf_rows, feat, de...  44.1 us
    pallas_call x1, Pallas kernels, per_device(): pl.pallas_call(functools.partial(near_kernel, leaves, leaf_rows), out_sha...  5.89 us
    unnamed x12, local copies, waits for them, and re-layouts  5.76 us

profile of v1, /device:TPU:2, one launch (start us, length us, event | category | flops | bytes accessed | tf_op | source)
XLA Modules:
  0.0 55.8 jit_solution(14779601336592557160)
XLA Ops:
  0.0 0.8 %copy.8.near_ref = s32[8,4]{1,0:T(8,128)S(1)} copy(s32[8,4]{0,1:T(4,128)} %param.9) | data formatting | bytes 256 | tf_op args[2]
  0.8 0.7 %copy.11 = s32[1,7,512]{2,1,0:T(8,128)S(1)} copy(s32[1,7,512]{2,0,1:T(1,128)} %param.12) | data formatting | bytes 28672
  1.5 0.0 copy-start
  1.5 1.0 %copy-done = bf16[4096,64]{0,1:T(8,128)(2,1)S(1)} copy-done((bf16[4096,64]{0,1:T(8,128)(2,1)S(1)}, bf16[4096,64]{0,1:T(8,128)(2,1)}, u32[]{:S(2)}) %copy-start) | copy-done | bytes 524312
  2.5 0.0 copy-start.1
  2.5 1.0 %copy-done.1 = bf16[4096,64]{0,1:T(8,128)(2,1)S(1)} copy-done((bf16[4096,64]{0,1:T(8,128)(2,1)S(1)}, bf16[4096,64]{0,1:T(8,128)(2,1)}, u32[]{:S(2)}) %copy-start.1) | copy-done | bytes 524312
  3.6 0.0 copy-start.2
  3.6 0.8 %copy-done.2 = s32[30,512]{1,0:T(8,128)S(1)} copy-done((s32[30,512]{1,0:T(8,128)S(1)}, s32[30,512]{1,0:T(8,128)}, u32[]{:S(2)}) %copy-start.2) | copy-done | bytes 61464
  4.4 0.0 copy-start.3
  4.4 0.7 %copy-done.3 = s32[8,512]{1,0:T(8,128)S(1)} copy-done((s32[8,512]{1,0:T(8,128)S(1)}, s32[8,512]{1,0:T(8,128)}, u32[]{:S(2)}) %copy-start.3) | copy-done | bytes 16408
  5.1 44.1 %tree.1 = (f32[64,4096]{1,0:T(8,128)S(1)}, bf16[3,64,4096]{2,1,0:T(8,128)(2,1)S(1)}, bf16[3,64,4096]{2,1,0:T(8,128)(2,1)S(1)}) custom-call(bf16[64,4096]{1,0:T(8,128)(2,1)S(1)} %bitcast.6, bf16[64,4096]{1,0:T(8,128)(2,1)S(1)} %bitcast.7, s32[8,512]{1,0:T(8,128)S(1)} %copy-done.3, s32[7,512]{1,0:T(8,128)S(1)} %bitcast.8, s32[30,512]{1,0:T(8,128)S(1)} %copy-done.2), custom_call_target="tpu_custom_call" | custom-call | tf_op jit(solution)/shard_map/tree/pallas_call | solution.py:329
  49.2 0.0 copy-start.4
  49.3 0.6 %copy-done.4 = s32[8]{0:T(128)S(1)} copy-done((s32[8]{0:T(128)S(1)}, s32[8]{0:T(128)}, u32[]{:S(2)}) %copy-start.4) | copy-done | bytes 56
  49.9 5.9 %near.1 = f32[64,4096]{1,0:T(8,128)} custom-call(s32[8,4]{1,0:T(8,128)S(1)} %copy.8.near_ref, s32[8]{0:T(128)S(1)} %copy-done.4, f32[64,4096]{1,0:T(8,128)S(1)} %get-tuple-element.8.part_ref, bf16[3,64,4096]{2,1,0:T(8,128)(2,1)S(1)} %get-tuple-element.9.winp_ref, bf16[3,64,4096]{2,1,0:T(8,128)(2,1)S(1)} %get-tuple-element.10.winw_ref), custom_call_target="tpu_custom_call" | custom-call | tf_op jit(solution)/shard_map/near/pallas_call | solution.py:355
Async XLA Ops:
  1.5 1.0 %copy-start = (bf16[4096,64]{0,1:T(8,128)(2,1)S(1)}, bf16[4096,64]{0,1:T(8,128)(2,1)}, u32[]{:S(2)}) copy-start(bf16[4096,64]{0,1:T(8,128)(2,1)} %param.7) | copy-start | bytes 1572868
  2.5 1.0 %copy-start.1 = (bf16[4096,64]{0,1:T(8,128)(2,1)S(1)}, bf16[4096,64]{0,1:T(8,128)(2,1)}, u32[]{:S(2)}) copy-start(bf16[4096,64]{0,1:T(8,128)(2,1)} %param.8) | copy-start | bytes 1572868
  3.6 0.8 %copy-start.2 = (s32[30,512]{1,0:T(8,128)S(1)}, s32[30,512]{1,0:T(8,128)}, u32[]{:S(2)}) copy-start(s32[30,512]{1,0:T(8,128)} %upper_ref.1) | copy-start | bytes 184324
  4.4 0.7 %copy-start.3 = (s32[8,512]{1,0:T(8,128)S(1)}, s32[8,512]{1,0:T(8,128)}, u32[]{:S(2)}) copy-start(s32[8,512]{1,0:T(8,128)} %leaf_ref.1) | copy-start | bytes 49156
  49.2 0.7 %copy-start.4 = (s32[8]{0:T(128)S(1)}, s32[8]{0:T(128)}, u32[]{:S(2)}) copy-start(s32[8]{0:T(128)} %count_ref.1) | copy-start | bytes 100
